TPU v7x, 512 devices: a whole 4x4x16 slice. The times are simulated.
512 devices in a mesh: cam: 8 (over y, x_lo), seq: 64 (over z, x_hi, core).
Axes of the slice: x: 4 (x_hi: 2, x_lo: 2; x = x_hi * 2 + x_lo), y: 4, z: 16, core: 2. Of those that a mesh axis runs over, the one named last changes fastest.
Arguments:
- query: bfloat16 [8, 384, 64, 1536], P('cam', 'seq'), may hold values from -5 to 5
- key: bfloat16 [8, 384, 64, 1536], P('cam', 'seq'), may hold values from -5 to 5
- value: bfloat16 [8, 384, 64, 1536], P('cam', 'seq'), may hold values from -6 to 6
- edge_cols: int32 [8], replicated, may hold values from 2 to 14, as said below
Outputs:
- mixed: bfloat16 [8, 384, 64, 1536], P('cam', 'seq')
Inputs may be any that keep to these rules, and one draw needn't show every extreme that they name: `edge_cols`: at least one pair has exactly 14 shared columns.
All inputs are finite; a program needn't handle non-finite values.
Results may differ from a plain program's by a relative error of at most 0.0045.
Values may be sent and summed in bfloat16 or wider, within the bound.
A program may use at most 128 MiB of HBM per device.

v0:
```python
import jax
import jax.numpy as jnp
from jax import lax
from jax.sharding import PartitionSpec as P

HD = 128
ROWS = 12
COLS = 32
MAX_COLS = 14


def shifted(value, axis, steps):
    count = lax.axis_size(axis)
    pairs = [(source, (source + steps) % count) for source in range(count)]
    return lax.ppermute(value, axis, pairs)


def attend(query_rows, key_rows, value_rows, valid):
    frames = query_rows.shape[0]
    count = query_rows.shape[1]
    heads = query_rows.shape[2] // HD
    q_four = query_rows.reshape(frames, count, heads, HD)
    k_four = key_rows.reshape(frames, key_rows.shape[1], heads, HD)
    v_four = value_rows.reshape(frames, value_rows.shape[1], heads, HD)
    scores = jnp.einsum(
        "fqhd,fkhd->fhqk", q_four, k_four, preferred_element_type=jnp.float32
    ) * HD ** (-0.5)
    if valid is not None:
        scores = jnp.where(valid[None, None, None, :], scores, -1e30)
    top = jnp.max(scores, axis=-1, keepdims=True)
    expo = jnp.exp(scores - top)
    weights = (expo / jnp.sum(expo, axis=-1, keepdims=True)).astype(jnp.bfloat16)
    result = jnp.einsum("fhqk,fkhd->fqhd", weights, v_four, preferred_element_type=jnp.float32)
    return result.reshape(frames, count, heads * HD)


def left_cols(frame_data):
    frames, width = (frame_data.shape[0], frame_data.shape[2])
    grid = frame_data.reshape(frames, ROWS, COLS, width)
    return grid[:, :, :MAX_COLS].reshape(frames, ROWS * MAX_COLS, width)


def right_cols(frame_data):
    frames, width = (frame_data.shape[0], frame_data.shape[2])
    grid = frame_data.reshape(frames, ROWS, COLS, width)
    return grid[:, :, COLS - MAX_COLS :].reshape(frames, ROWS * MAX_COLS, width)


def flatten(shard):
    return shard.reshape(shard.shape[1], shard.shape[2] * shard.shape[3])


def frame_major(gathered, width):
    total_rows = gathered.shape[0]
    frames = gathered.shape[1] // width
    return gathered.reshape(total_rows, frames, width).transpose(1, 0, 2)


def local(query, key, value, edge_cols):
    cams = lax.axis_size("cam")
    here = lax.axis_index("cam")
    width = query.shape[3]
    all_frames = query.shape[2]
    cycle = lax.iota(jnp.int32, cams)
    width_right = jnp.sum(jnp.where(cycle == here, edge_cols, 0))
    width_left = jnp.sum(jnp.where(cycle == (here + cams - 1) % cams, edge_cols, 0))
    column = jnp.tile(lax.iota(jnp.int32, MAX_COLS), ROWS)
    right_own = column >= MAX_COLS - width_right
    right_next = column < width_right
    left_prior = column >= MAX_COLS - width_left
    left_own = column < width_left
    flat_q, flat_k, flat_v = (
        lax.all_to_all(flatten(query), "seq", split_axis=1, concat_axis=0, tiled=True),
        lax.all_to_all(flatten(key), "seq", split_axis=1, concat_axis=0, tiled=True),
        lax.all_to_all(flatten(value), "seq", split_axis=1, concat_axis=0, tiled=True),
    )
    q_here = frame_major(flat_q, width)
    k_here = frame_major(flat_k, width)
    v_here = frame_major(flat_v, width)
    next_kl, next_vl = shifted((left_cols(k_here), left_cols(v_here)), "cam", -1)
    prior_kr, prior_vr = shifted((right_cols(k_here), right_cols(v_here)), "cam", 1)
    frames = q_here.shape[0]
    tokens_frame = q_here.shape[1]
    spatial = attend(q_here, k_here, v_here, None)
    right_out = attend(
        right_cols(q_here),
        jnp.concatenate([right_cols(k_here), next_kl], axis=1),
        jnp.concatenate([right_cols(v_here), next_vl], axis=1),
        jnp.concatenate([right_own, right_next]),
    )
    right_out = right_out * right_own[None, :, None].astype(jnp.float32)
    left_out = attend(
        left_cols(q_here),
        jnp.concatenate([prior_kr, left_cols(k_here)], axis=1),
        jnp.concatenate([prior_vr, left_cols(v_here)], axis=1),
        jnp.concatenate([left_prior, left_own]),
    )
    left_out = left_out * left_own[None, :, None].astype(jnp.float32)
    total = spatial.reshape(frames, ROWS, COLS, width)
    total = total.at[:, :, :MAX_COLS].add(left_out.reshape(frames, ROWS, MAX_COLS, width))
    total = total.at[:, :, COLS - MAX_COLS :].add(right_out.reshape(frames, ROWS, MAX_COLS, width))
    outgoing = total.reshape(frames, tokens_frame, width).astype(jnp.bfloat16)
    outgoing = outgoing.transpose(1, 0, 2).reshape(tokens_frame, frames * width)
    returned = lax.all_to_all(outgoing, "seq", split_axis=0, concat_axis=1, tiled=True)
    return returned.reshape(1, returned.shape[0], all_frames, width)


def solution(mesh):
    return jax.shard_map(
        local,
        mesh=mesh,
        in_specs=(
            P("cam", "seq", None, None),
            P("cam", "seq", None, None),
            P("cam", "seq", None, None),
            P(),
        ),
        out_specs=P("cam", "seq", None, None),
        check_vma=False,
    )
```

profile of v0, /device:TPU:1, one launch (start us, length us, event | category | flops | bytes accessed | tf_op | source)
XLA Modules:
  0.0 442.8 jit_solution(3002953051390250589)
XLA Ops:
  0.0 3.2 copy.79
  3.2 19.6 %all-to-all-start = ((bf16[6,64,1536]{2,0,1:T(8,128)(2,1)}), bf16[6,64,1536]{2,0,1:T(8,128)(2,1)S(1)}, u32[]{:S(2)}, u32[]{:S(2)}) async-start(bf16[6,64,1536]{2,0,1:T(8,128)(2,1)} %bitcast.88), calls=%async_computation | async-start | bytes 3145728 | tf_op jit(solution)/shard_map/all_to_all | solution.py:73
  22.8 1.8 copy.78
  24.6 74.6 %all-to-all-done = bf16[6,64,1536]{2,0,1:T(8,128)(2,1)S(1)} async-done(((bf16[6,64,1536]{2,0,1:T(8,128)(2,1)}), bf16[6,64,1536]{2,0,1:T(8,128)(2,1)S(1)}, u32[]{:S(2)}, u32[]{:S(2)}) %all-to-all-start) | async-done | bytes 1179680 | tf_op jit(solution)/shard_map/all_to_all | solution.py:73
  99.2 7.5 %all-to-all-start.1 = ((bf16[6,64,1536]{2,0,1:T(8,128)(2,1)}), bf16[6,64,1536]{2,0,1:T(8,128)(2,1)S(1)}, u32[]{:S(2)}, u32[]{:S(2)}) async-start(bf16[6,64,1536]{2,0,1:T(8,128)(2,1)} %bitcast.96), calls=%async_computation.1 | async-start | bytes 3145728 | tf_op jit(solution)/shard_map/all_to_all | solution.py:74
  106.7 3.1 copy.77
  109.8 73.3 %all-to-all-done.1 = bf16[6,64,1536]{2,0,1:T(8,128)(2,1)S(1)} async-done(((bf16[6,64,1536]{2,0,1:T(8,128)(2,1)}), bf16[6,64,1536]{2,0,1:T(8,128)(2,1)S(1)}, u32[]{:S(2)}, u32[]{:S(2)}) %all-to-all-start.1) | async-done | bytes 1179680 | tf_op jit(solution)/shard_map/all_to_all | solution.py:74
  183.2 1.2 copy-done
  184.3 7.5 %all-to-all-start.2 = ((bf16[6,64,1536]{2,0,1:T(8,128)(2,1)}), bf16[6,64,1536]{2,0,1:T(8,128)(2,1)S(1)}, u32[]{:S(2)}, u32[]{:S(2)}) async-start(bf16[6,64,1536]{2,0,1:T(8,128)(2,1)} %bitcast.95), calls=%async_computation.2 | async-start | bytes 3145728 | tf_op jit(solution)/shard_map/all_to_all | solution.py:75
  191.8 0.6 fusion.51
  193.8 1.2 iota_compare_fusion
  195.3 0.6 pad_add_fusion
  196.0 0.6 fusion.47
  196.6 1.3 reshape_transpose_reshape.8
  197.9 2.3 reshape.308
  200.1 3.2 reshape_transpose_reshape.7
  203.3 2.3 reshape.309
  205.6 1.4 fusion.65
  207.0 1.0 reshape.313
  208.4 0.9 reshape.319
  209.3 1.3 concatenate.47
  210.7 57.5 %all-to-all-done.2 = bf16[6,64,1536]{2,0,1:T(8,128)(2,1)S(1)} async-done(((bf16[6,64,1536]{2,0,1:T(8,128)(2,1)}), bf16[6,64,1536]{2,0,1:T(8,128)(2,1)S(1)}, u32[]{:S(2)}, u32[]{:S(2)}) %all-to-all-start.2) | async-done | bytes 1179680 | tf_op jit(solution)/shard_map/all_to_all | solution.py:75
  268.6 2.4 reshape.310
  271.1 0.9 reshape.311
  272.1 1.3 concatenate.49
  273.4 0.9 reshape.317
  274.3 1.3 concatenate.43
  275.7 1.2 fusion.63
  276.9 2.4 reshape.321
  279.3 2.4 reshape.315
  281.7 0.9 copy.49
  282.7 0.9 copy.43
  283.6 4.7 %collective-permute-start.3 = (bf16[1,168,1536]{2,1,0:T(8,128)(2,1)}, bf16[1,168,1536]{2,1,0:T(8,128)(2,1)}, u32[]{:S(2)}, u32[]{:S(2)}) collective-permute-start(bf16[1,168,1536]{2,1,0:T(8,128)(2,1)} %reshape.319), channel_id=1, source_target_pairs={{0,448},{64,0},{128,64},{192,128},{256,192},{320,256},{384,320},{4... | collective-permute-start | bytes 1548296 | tf_op jit(solution)/shard_map/ppermute | solution.py:15
  288.3 1.9 collective-permute-start.1
  290.2 0.9 copy.47
  291.1 0.9 copy.41
  292.1 5.5 %collective-permute-start.2 = (bf16[1,168,1536]{2,1,0:T(8,128)(2,1)}, bf16[1,168,1536]{2,1,0:T(8,128)(2,1)}, u32[]{:S(2)}, u32[]{:S(2)}) collective-permute-start(bf16[1,168,1536]{2,1,0:T(8,128)(2,1)} %reshape.317), channel_id=1, source_target_pairs={{0,448},{64,0},{128,64},{192,128},{256,192},{320,256},{384,320},{4... | collective-permute-start | bytes 1548296 | tf_op jit(solution)/shard_map/ppermute | solution.py:15
  297.5 2.1 collective-permute-start
  299.7 1.2 fusion.28
  300.9 2.9 copy-done.2
  303.8 1.8 fusion.66
  305.6 8.2 %fusion.16 = f32[1,384,12,128]{3,1,2,0:T(8,128)S(1)} fusion(f32[12,384]{1,0:T(8,128)S(1)} %fusion.66, bf16[384,12,128]{2,1,0:T(8,128)(2,1)} %reshape.310, f32[12,384,384]{1,2,0:T(8,128)} %copy-done.2), kind=kOutput, calls=%fused_computation.21 | convolution fusion | flops 461837184 | bytes 10635264 | tf_op jit(solution)/shard_map/fhqk,fkhd->fqhd/dot_general | solution.py:33
  313.8 3.1 copy.39
  316.9 2.7 reshape_reshape.2
  319.7 1.1 copy_bitcast_fusion.3
  320.8 1.9 fusion.38
  322.7 1.3 fusion.68
  324.1 1.1 copy_bitcast_fusion.4
  325.2 1.0 fusion.25
  326.3 1.1 copy_bitcast_fusion.5
  327.4 2.5 fusion.33
  329.9 1.3 copy.52
  331.2 1.5 reshape.325
  332.7 4.2 fusion.67
  336.9 1.1 copy_bitcast_fusion.6
  338.1 1.0 fusion.26
  339.1 1.3 copy.45
  340.4 2.4 reshape.324
  342.8 2.5 slice_add_fusion.1
  345.3 4.6 %scatter-add.6 = f32[1,12,32,1536]{3,2,1,0:T(8,128)S(1)} dynamic-update-slice(f32[1,12,32,1536]{3,2,1,0:T(8,128)S(1)} %reshape_reshape.2, f32[1,12,14,1536]{3,2,1,0:T(8,128)} %slice_add_fusion.1, s32[]{:T(128)} %constant.84.clone.1, s32[]{:T(128)} %constant.84.clone.1, s32[]{:T(128)} %constant.84.clone.1, s32[]{:T(128)} %constant.84.clone.1) | dynamic-update-slice | bytes 2064388 | tf_op jit(solution)/shard_map/scatter-add | solution.py:100
  349.9 1.2 slice_add_fusion
  351.1 4.5 %scatter-add.9 = f32[1,12,32,1536]{3,2,1,0:T(8,128)S(1)} dynamic-update-slice(f32[1,12,32,1536]{3,2,1,0:T(8,128)S(1)} %scatter-add.6, f32[1,12,14,1536]{3,2,1,0:T(8,128)} %slice_add_fusion, s32[]{:T(128)} %constant.84.clone.1, s32[]{:T(128)} %constant.84.clone.1, s32[]{:T(128)} %constant.87.clone.1, s32[]{:T(128)} %constant.84.clone.1) | dynamic-update-slice | bytes 2064388 | tf_op jit(solution)/shard_map/scatter-add | solution.py:101
  356.2 85.2 %all_to_all.61 = bf16[64,6,1536]{2,1,0:T(8,128)(2,1)S(1)} all-to-all(bf16[64,6,1536]{2,1,0:T(8,128)(2,1)S(1)} %convert_element_type.44), channel_id=1, replica_groups=mesh['cam'=8,'seq'=64] {'seq'}, dimensions={0} | all-to-all | bytes 2359296 | tf_op jit(solution)/shard_map/all_to_all | solution.py:104
  441.5 1.4 copy.54
  (46 shorter events, 2.1 us)
Async XLA Ops:
  0.0 22.8 %copy-start.12 = (bf16[1,6,64,1536]{3,2,1,0:T(8,128)(2,1)S(1)}, bf16[1,6,64,1536]{3,2,1,0:T(8,128)(2,1)}, u32[]{:S(2)}) copy-start(bf16[1,6,64,1536]{3,2,1,0:T(8,128)(2,1)} %param.9) | copy-start | bytes 3538948
  3.2 96.0 %all-to-all-start = ((bf16[6,64,1536]{2,0,1:T(8,128)(2,1)}), bf16[6,64,1536]{2,0,1:T(8,128)(2,1)S(1)}, u32[]{:S(2)}, u32[]{:S(2)}) async-start(bf16[6,64,1536]{2,0,1:T(8,128)(2,1)} %bitcast.88), calls=%async_computation | async-start | bytes 3145728 | tf_op jit(solution)/shard_map/all_to_all | solution.py:73
  99.2 83.9 %all-to-all-start.1 = ((bf16[6,64,1536]{2,0,1:T(8,128)(2,1)}), bf16[6,64,1536]{2,0,1:T(8,128)(2,1)S(1)}, u32[]{:S(2)}, u32[]{:S(2)}) async-start(bf16[6,64,1536]{2,0,1:T(8,128)(2,1)} %bitcast.96), calls=%async_computation.1 | async-start | bytes 3145728 | tf_op jit(solution)/shard_map/all_to_all | solution.py:74
  106.7 85.1 %copy-start.15 = (s32[8]{0:T(128)S(1)}, s32[8]{0:T(128)}, u32[]{:S(2)}) copy-start(s32[8]{0:T(128)} %param.11) | copy-start | bytes 100
  183.2 1.2 copy-start
  184.3 83.9 %all-to-all-start.2 = ((bf16[6,64,1536]{2,0,1:T(8,128)(2,1)}), bf16[6,64,1536]{2,0,1:T(8,128)(2,1)S(1)}, u32[]{:S(2)}, u32[]{:S(2)}) async-start(bf16[6,64,1536]{2,0,1:T(8,128)(2,1)} %bitcast.95), calls=%async_computation.2 | async-start | bytes 3145728 | tf_op jit(solution)/shard_map/all_to_all | solution.py:75
  200.1 3.2 copy-start.1
  271.1 4.5 %copy-start.5 = (bf16[1,12,32,1536]{3,2,1,0:T(8,128)(2,1)S(1)}, bf16[1,12,32,1536]{3,2,1,0:T(8,128)(2,1)}, u32[]{:S(2)}) copy-start(bf16[1,12,32,1536]{3,2,1,0:T(8,128)(2,1)} %reshape_transpose_reshape.8) | copy-start | bytes 3538948
  276.9 5.8 %copy-start.6 = (bf16[1,168,12,128]{3,2,1,0:T(8,128)(2,1)S(1)}, bf16[1,168,12,128]{3,2,1,0:T(8,128)(2,1)}, u32[]{:S(2)}) copy-start(bf16[1,168,12,128]{3,2,1,0:T(8,128)(2,1)} %concatenate.47) | copy-start | bytes 1548292
  276.9 13.3 %copy-start.7 = (bf16[1,168,12,128]{3,2,1,0:T(8,128)(2,1)S(1)}, bf16[1,168,12,128]{3,2,1,0:T(8,128)(2,1)}, u32[]{:S(2)}) copy-start(bf16[1,168,12,128]{3,2,1,0:T(8,128)(2,1)} %concatenate.49) | copy-start | bytes 1548292
  279.3 11.8 %copy-start.8 = (bf16[1,168,12,128]{3,2,1,0:T(8,128)(2,1)S(1)}, bf16[1,168,12,128]{3,2,1,0:T(8,128)(2,1)}, u32[]{:S(2)}) copy-start(bf16[1,168,12,128]{3,2,1,0:T(8,128)(2,1)} %concatenate.43) | copy-start | bytes 1548292
  281.7 17.9 %copy-start.3 = (bf16[384,12,128]{2,1,0:T(8,128)(2,1)S(1)}, bf16[384,12,128]{2,1,0:T(8,128)(2,1)}, u32[]{:S(2)}) copy-start(bf16[384,12,128]{2,1,0:T(8,128)(2,1)} %reshape.308) | copy-start | bytes 3538948
  281.7 18.0 %copy-start.4 = (bf16[384,12,128]{2,1,0:T(8,128)(2,1)S(1)}, bf16[384,12,128]{2,1,0:T(8,128)(2,1)}, u32[]{:S(2)}) copy-start(bf16[384,12,128]{2,1,0:T(8,128)(2,1)} %reshape.309) | copy-start | bytes 3538948
  283.6 36.0 %collective-permute-start.3 = (bf16[1,168,1536]{2,1,0:T(8,128)(2,1)}, bf16[1,168,1536]{2,1,0:T(8,128)(2,1)}, u32[]{:S(2)}, u32[]{:S(2)}) collective-permute-start(bf16[1,168,1536]{2,1,0:T(8,128)(2,1)} %reshape.319), channel_id=1, source_target_pairs={{0,448},{64,0},{128,64},{192,128},{256,192},{320,256},{384,320},{4... | collective-permute-start | bytes 1548296 | tf_op jit(solution)/shard_map/ppermute | solution.py:15
  288.3 38.0 %collective-permute-start.1 = (bf16[1,168,1536]{2,1,0:T(8,128)(2,1)}, bf16[1,168,1536]{2,1,0:T(8,128)(2,1)}, u32[]{:S(2)}, u32[]{:S(2)}) collective-permute-start(bf16[1,168,1536]{2,1,0:T(8,128)(2,1)} %reshape.313), channel_id=1, source_target_pairs={{0,64},{64,128},{128,192},{192,256},{256,320},{320,384},{384,448},... | collective-permute-start | bytes 1548296 | tf_op jit(solution)/shard_map/ppermute | solution.py:15
  292.1 32.0 %collective-permute-start.2 = (bf16[1,168,1536]{2,1,0:T(8,128)(2,1)}, bf16[1,168,1536]{2,1,0:T(8,128)(2,1)}, u32[]{:S(2)}, u32[]{:S(2)}) collective-permute-start(bf16[1,168,1536]{2,1,0:T(8,128)(2,1)} %reshape.317), channel_id=1, source_target_pairs={{0,448},{64,0},{128,64},{192,128},{256,192},{320,256},{384,320},{4... | collective-permute-start | bytes 1548296 | tf_op jit(solution)/shard_map/ppermute | solution.py:15
  297.5 39.4 %collective-permute-start = (bf16[1,168,1536]{2,1,0:T(8,128)(2,1)}, bf16[1,168,1536]{2,1,0:T(8,128)(2,1)}, u32[]{:S(2)}, u32[]{:S(2)}) collective-permute-start(bf16[1,168,1536]{2,1,0:T(8,128)(2,1)} %reshape.311), channel_id=1, source_target_pairs={{0,64},{64,128},{128,192},{192,256},{256,320},{320,384},{384,448},... | collective-permute-start | bytes 1548296 | tf_op jit(solution)/shard_map/ppermute | solution.py:15
  300.9 2.9 copy-start.2
  316.9 3.9 copy-start.10
  322.7 2.5 copy-start.14
  325.2 2.2 copy-start.9
  325.2 2.2 copy-start.11
  332.7 5.4 %copy-start.13 = (bf16[1,168,12,128]{3,1,2,0:T(8,128)(2,1)S(1)}, bf16[1,168,12,128]{3,1,2,0:T(8,128)(2,1)}, u32[]{:S(2)}) copy-start(bf16[1,168,12,128]{3,1,2,0:T(8,128)(2,1)} %copy.41) | copy-start | bytes 1548292
where the time goes:
time: 446 us; the launch traced here: 443 us
  waiting for transfers between devices  205 us (46%)
  blocking collectives  85.2 us (19%)
  local copies, waits for them, and re-layouts  71.6 us (16%)
  starting transfers between devices  48.8 us (11%)
  matrix products  15.8 us (4%)
  other arithmetic  14.3 us (3%)
    all_to_all x1, blocking collectives, local(): lax.all_to_all(outgoing, 'seq', split_axis=0, concat_axis=1, tiled=True)  85.2 us
    all_to_all x1, waiting for transfers between devices, local(): lax.all_to_all(flatten(query), 'seq', split_axis=1, concat_axis=0, tiled=...  74.6 us
    all_to_all x1, waiting for transfers between devices, local(): lax.all_to_all(flatten(key), 'seq', split_axis=1, concat_axis=0, tiled=True)  73.3 us
    all_to_all x1, waiting for transfers between devices, local(): lax.all_to_all(flatten(value), 'seq', split_axis=1, concat_axis=0, tiled=...  57.5 us
    all_to_all x1, starting transfers between devices, local(): lax.all_to_all(flatten(query), 'seq', split_axis=1, concat_axis=0, tiled=...  19.6 us
    ppermute x4, starting transfers between devices, shifted(): return lax.ppermute(value, axis, pairs)  14.2 us
    unnamed x35, local copies, waits for them, and re-layouts  12.2 us
    another operation x5, local copies, waits for them, and re-layouts  11.7 us
  transfers between devices with their start and end apart: 7, of which 3 were waited for; matrix products, arithmetic and copies ran while one was open for 13% of the time, Pallas kernels for 0%

commit v1 on v0

v1 whole, which is shorter than its diff:
```python
import jax
import jax.numpy as jnp
from jax import lax
from jax.experimental import pallas as pl
from jax.experimental.pallas import tpu as pltpu
from jax.sharding import PartitionSpec as P

MESH = pl.DeviceIdType.MESH
HD = 128
COLS = 32
MAX_COLS = 14
BF = jnp.bfloat16
F32 = jnp.float32
NZ = 16
NG = 4
BLK = 6
FR = 16
HEADS = 3
FG = 4
PER = 4
POS = NZ * BLK
EDGE = 48
MID = 16
ROWS_G = 2 * EDGE + MID
AHEAD = 2
SCALE = HD**-0.5 * 1.4426950408889634


def tables():
    slots, cols, counts = [], [], []
    for g in range(NG):
        left, right, mid = [], [], []
        for b in range(PER):
            for i in range(BLK):
                col = (PER * BLK * b + BLK * g + i) % COLS
                entry = (BLK * b + i, col)
                (left if col < MAX_COLS else right if col >= COLS - MAX_COLS else mid).append(entry)
        groups = [left, right, mid]
        counts.append([len(x) for x in groups])
        row_s, row_c = [], []
        for x, room in zip(groups, (EDGE // 4, EDGE // 4, MID // 4)):
            for k in range(room):
                row_s.append(x[k][0] if k < len(x) else x[0][0])
                row_c.append(x[k][1] if k < len(x) else -1)
        slots.append(row_s)
        cols.append(row_c)
    return slots, cols, counts


SLOTS, COLUMNS, COUNTS = tables()
KINDS = len(SLOTS[0])


def by_g(g, values):
    if len(set(values)) == 1:
        return values[0]
    out = jnp.int32(values[-1])
    for n in range(len(values) - 2, -1, -1):
        out = jnp.where(g == n, jnp.int32(values[n]), out)
    return out


def dot(a, b, dims):
    return lax.dot_general(a, b, (dims, ((), ())), preferred_element_type=F32)


def kernel(
    edge_ref, q_ref, k_ref, v_ref, out_ref,
    rxz, st2, rx2, edges, ost, rxo, otx, perm, ones, bias, qvalid,
    z_send, z_recv, g_send, g_recv, e_send, e_recv, og_send, og_recv, oz_send, oz_recv,
):
    cam = lax.axis_index("cam")
    seq = lax.axis_index("seq")
    cams = lax.axis_size("cam")
    z = seq // NG
    g = seq % NG
    prior = lax.rem(cam + cams - 1, cams)
    after = lax.rem(cam + 1, cams)
    hg, fg = z // 4, z % 4
    args = (k_ref, v_ref, q_ref)

    def ring(d):
        return lax.rem(z + d, NZ)

    bar = pltpu.get_barrier_semaphore()

    def greet(dev):
        pl.semaphore_signal(bar, inc=1, device_id=dev, device_id_type=MESH)

    @pl.loop(1, NZ)
    def _(d):
        greet((cam, ring(d) * NG + g))

    for d in range(1, NG):
        greet((cam, z * NG + lax.rem(g + d, NG)))
    for d in range(NG):
        greet((prior, z * NG + d))
        greet((after, z * NG + d))
    pl.semaphore_wait(bar, NZ - 1 + NG - 1 + 2 * NG)

    def z_src(t, h, zt):
        rows = pl.ds(pl.multiple_of((zt % 4) * FR, FR), FR)
        lanes = pl.ds(pl.multiple_of(((zt // 4) * HEADS + h) * HD, HD), HD)
        return args[t].at[:, rows, lanes]

    def z_issue(t, h):
        dst = rxz.at[t, h, pl.ds(z * BLK, BLK)]

        def go(d):
            zt = ring(d)
            pltpu.make_async_remote_copy(
                z_src(t, h, zt), dst, z_send.at[t, h], z_recv.at[t, h],
                device_id=(cam, zt * NG + g), device_id_type=MESH,
            ).start()

        @pl.loop(1, NZ // 2)
        def _(d):
            go(d)
            go(NZ - d)

        go(NZ // 2)
        pltpu.make_async_copy(z_src(t, h, z), dst, z_recv.at[t, h]).start()

    def wait_bytes(ref, sem):
        pltpu.make_async_copy(ref, ref, sem).wait()

    z_issue(0, 0)
    z_issue(1, 0)

    r = lax.broadcasted_iota(jnp.int32, (256, 256), 0)
    c = lax.broadcasted_iota(jnp.int32, (256, 256), 1)
    hit = c == (r % 16) * 16 + r // 16
    perm[0] = jnp.where(hit, 1.0, 0.0).astype(BF)
    perm[1] = jnp.where(jnp.logical_and(hit, r % 16 < 8), 1.0, 0.0).astype(BF)

    def column_of(idx, kind):
        dev, k = idx // EDGE, (idx % EDGE) // 4
        col = jnp.full(idx.shape, -1, jnp.int32)
        for n in range(NG):
            for kk in range(COUNTS[n][kind]):
                here = jnp.logical_and(dev == n, k == kk)
                col = jnp.where(here, COLUMNS[n][kind * (EDGE // 4) + kk], col)
        return col

    w_right = edge_ref[cam]
    w_left = edge_ref[prior]

    def on_left(col, w):
        return jnp.logical_and(col >= 0, col < w)

    def on_right(col, w):
        return col >= COLS - w

    lane = lax.broadcasted_iota(jnp.int32, (8, NG * EDGE), 1)
    col_l, col_r = column_of(lane, 0), column_of(lane, 1)

    def as_bias(ok):
        return jnp.where(ok, 0.0, -1e30).astype(F32)

    bias[0] = jnp.concatenate([as_bias(on_right(col_r, w_left)), as_bias(on_left(col_l, w_left))], axis=1)
    bias[1] = jnp.concatenate([as_bias(on_right(col_r, w_right)), as_bias(on_left(col_l, w_right))], axis=1)
    row = lax.broadcasted_iota(jnp.int32, (NG * EDGE, HD), 0)
    qvalid[0] = jnp.where(on_left(column_of(row, 0), w_left), 1.0, 0.0).astype(F32)
    qvalid[1] = jnp.where(on_right(column_of(row, 1), w_right), 1.0, 0.0).astype(F32)
    for n in range(NG):
        for kind, (base, room) in enumerate(((0, EDGE), (NG * EDGE, EDGE), (2 * NG * EDGE, MID))):
            at = lax.broadcasted_iota(jnp.int32, (room, HD), 0)
            ones[base + n * room : base + (n + 1) * room] = jnp.where(at < 4 * COUNTS[n][kind], 1.0, 0.0).astype(BF)

    slot = [by_g(g, [SLOTS[n][k] for n in range(NG)]) for k in range(KINDS)]
    room_of = [(0, k) for k in range(EDGE // 4)] + [(1, k) for k in range(EDGE // 4)] + [(2, k) for k in range(MID // 4)]
    real = [by_g(g, [1 if k < COUNTS[n][kind] else 0 for n in range(NG)]) for kind, k in room_of]

    def place(k, a):
        if isinstance(real[k], int):
            return PER * BLK * a + slot[k]
        return jnp.where(real[k] == 1, PER * BLK * a + slot[k], POS)

    def to_frames(t, h, zero_pads):
        for j in range(KINDS // 4):
            tiles = []
            for k in range(4 * j, 4 * j + 4):
                for a in range(4):
                    tiles.append(rxz[t, h, PER * BLK * a + slot[k]])
            x = jnp.concatenate(tiles, axis=0)
            last = real[4 * j + 3]
            which = 0 if (isinstance(last, int) or not zero_pads) else 1 - last
            y = dot(perm[which], x, ((1,), (0,)))
            st2[t, h, :, 16 * j : 16 * j + 16, :] = y.astype(BF).reshape(FR, 16, HD)

    def to_tiles(h):
        for j in range(KINDS // 4):
            x = rxo[h, :, 16 * j : 16 * j + 16, :].reshape(256, HD)
            y = dot(perm[0], x, ((1,), (0,))).astype(BF).reshape(16, FR, HD)
            for n in range(16):
                otx[h, place(4 * j + n // 4, n % 4)] = y[n]

    def g_issue(t, h, with_edges):
        for d in (2, 1, 3):
            gt = lax.rem(g + d, NG)
            pltpu.make_async_remote_copy(
                st2.at[t, h, pl.ds(gt * FG, FG)], rx2.at[t, h, g], g_send.at[t, h], g_recv.at[t, h],
                device_id=(cam, z * NG + gt), device_id_type=MESH,
            ).start()
        pltpu.make_async_copy(st2.at[t, h, pl.ds(g * FG, FG)], rx2.at[t, h, g], g_recv.at[t, h]).start()
        if with_edges:
            for d in range(NG):
                gt = lax.rem(g + d, NG)
                for side, who, base in ((0, after, EDGE), (1, prior, 0)):
                    pltpu.make_async_remote_copy(
                        st2.at[t, h, pl.ds(gt * FG, FG), pl.ds(base, EDGE)], edges.at[t, h, side, g],
                        e_send.at[t, h], e_recv.at[t, h],
                        device_id=(who, z * NG + gt), device_id_type=MESH,
                    ).start()

    def arrive(t, h, zero_pads, with_edges):
        wait_bytes(rxz.at[t, h], z_recv.at[t, h])
        nt = (t + AHEAD) % 3
        if t + AHEAD < 3:
            z_issue(nt, h)
        else:
            @pl.when(h < HEADS - 1)
            def _():
                z_issue(nt, h + 1)
        to_frames(t, h, zero_pads)
        g_issue(t, h, with_edges)

    def weigh(q, k, v, extra):
        s = dot(q, k, ((1,), (1,))) * SCALE
        if extra is not None:
            s = s + extra
        p = jnp.exp2(s - jnp.max(s, axis=-1, keepdims=True)).astype(BF)
        acc = dot(p, v, ((1,), (0,)))
        return acc[:, :HD] / acc[:, HD:]

    def gather(t, h, f, lo, n):
        return jnp.concatenate([rx2[t, h, gs, f, lo : lo + n, :] for gs in range(NG)], axis=0)

    def edge(t, h, f, side):
        return jnp.concatenate([edges[t, h, side, gs, f] for gs in range(NG)], axis=0)

    def attend(h):
        for t in range(3):
            wait_bytes(rx2.at[t, h], g_recv.at[t, h])
        for t in range(2):
            wait_bytes(edges.at[t, h], e_recv.at[t, h])

        @pl.loop(0, FG)
        def _(f):
            kl, kr, km = gather(0, h, f, 0, EDGE), gather(0, h, f, EDGE, EDGE), gather(0, h, f, 2 * EDGE, MID)
            vl, vr, vm = gather(1, h, f, 0, EDGE), gather(1, h, f, EDGE, EDGE), gather(1, h, f, 2 * EDGE, MID)
            ql, qr, qm = gather(2, h, f, 0, EDGE), gather(2, h, f, EDGE, EDGE), gather(2, h, f, 2 * EDGE, MID)
            k_all = jnp.concatenate([kl, kr, km], axis=0)
            v_all = jnp.concatenate([jnp.concatenate([vl, vr, vm], axis=0), ones[...]], axis=1)
            full = jnp.full((2 * NG * EDGE, HD), 1.0, BF)
            k_left = jnp.concatenate([edge(0, h, f, 0), kl], axis=0)
            v_left = jnp.concatenate([jnp.concatenate([edge(1, h, f, 0), vl], axis=0), full], axis=1)
            k_right = jnp.concatenate([kr, edge(0, h, f, 1)], axis=0)
            v_right = jnp.concatenate([jnp.concatenate([vr, edge(1, h, f, 1)], axis=0), full], axis=1)
            o_l = weigh(ql, k_all, v_all, None) + weigh(ql, k_left, v_left, bias[0, 0:1]) * qvalid[0]
            o_r = weigh(qr, k_all, v_all, None) + weigh(qr, k_right, v_right, bias[1, 0:1]) * qvalid[1]
            o_m = weigh(qm, k_all, v_all, None)
            o_l, o_r, o_m = o_l.astype(BF), o_r.astype(BF), o_m.astype(BF)
            for n in range(NG):
                ost[h, n, f, 0:EDGE, :] = o_l[n * EDGE : (n + 1) * EDGE]
                ost[h, n, f, EDGE : 2 * EDGE, :] = o_r[n * EDGE : (n + 1) * EDGE]
                ost[h, n, f, 2 * EDGE :, :] = o_m[n * MID : (n + 1) * MID]
            for d in (2, 1, 3):
                gt = lax.rem(g + d, NG)
                pltpu.make_async_remote_copy(
                    ost.at[h, gt, f], rxo.at[h, g * FG + f], og_send.at[h], og_recv.at[h],
                    device_id=(cam, z * NG + gt), device_id_type=MESH,
                ).start()
            pltpu.make_async_copy(ost.at[h, g, f], rxo.at[h, g * FG + f], og_recv.at[h]).start()

    def give_back(h):
        wait_bytes(rxo.at[h], og_recv.at[h])
        to_tiles(h)
        dst = out_ref.at[:, pl.ds(pl.multiple_of(fg * FR, FR), FR), pl.ds(pl.multiple_of((hg * HEADS + h) * HD, HD), HD)]

        def go(d):
            zt = ring(d)
            pltpu.make_async_remote_copy(
                otx.at[h, pl.ds(zt * BLK, BLK)], dst, oz_send.at[h], oz_recv.at[h],
                device_id=(cam, zt * NG + g), device_id_type=MESH,
            ).start()

        @pl.loop(1, NZ // 2)
        def _(d):
            go(d)
            go(NZ - d)

        go(NZ // 2)
        pltpu.make_async_copy(otx.at[h, pl.ds(z * BLK, BLK)], dst, oz_recv.at[h]).start()

    @pl.loop(0, HEADS)
    def _(h):
        arrive(0, h, False, True)

        @pl.when(h > 0)
        def _():
            attend(h - 1)

        arrive(1, h, True, True)

        @pl.when(h == HEADS - 1)
        def _():
            @pl.loop(0, HEADS - 1)
            def _(hh):
                give_back(hh)

        arrive(2, h, False, False)

    attend(HEADS - 1)
    give_back(HEADS - 1)

    @pl.loop(0, HEADS)
    def _(h):
        for t in range(3):
            wait_bytes(rxz.at[t, h, pl.ds(0, (NZ - 1) * BLK)], z_send.at[t, h])
            wait_bytes(rx2.at[t, h, pl.ds(0, NG - 1)], g_send.at[t, h])
        for t in range(2):
            wait_bytes(edges.at[t, h], e_send.at[t, h])
        wait_bytes(rx2.at[0, h, pl.ds(0, NG - 1)], og_send.at[h])
        wait_bytes(rxz.at[0, h, pl.ds(0, (NZ - 1) * BLK)], oz_send.at[h])
        wait_bytes(rxz.at[0, h], oz_recv.at[h])


def local(query, key, value, edge_cols):
    dma = pltpu.SemaphoreType.DMA
    out = pl.pallas_call(
        kernel,
        out_shape=jax.ShapeDtypeStruct(query.shape[1:], query.dtype),
        in_specs=[pl.BlockSpec(memory_space=pltpu.SMEM)] + [pl.BlockSpec(memory_space=pl.ANY)] * 3,
        out_specs=pl.BlockSpec(memory_space=pl.ANY),
        scratch_shapes=[
            pltpu.VMEM((3, HEADS, POS, FR, HD), BF),
            pltpu.VMEM((3, HEADS, FR, ROWS_G, HD), BF),
            pltpu.VMEM((3, HEADS, NG, FG, ROWS_G, HD), BF),
            pltpu.VMEM((2, HEADS, 2, NG, FG, EDGE, HD), BF),
            pltpu.VMEM((HEADS, NG, FG, ROWS_G, HD), BF),
            pltpu.VMEM((HEADS, FR, ROWS_G, HD), BF),
            pltpu.VMEM((HEADS, POS + 1, FR, HD), BF),
            pltpu.VMEM((2, 256, 256), BF),
            pltpu.VMEM((NG * ROWS_G, HD), BF),
            pltpu.VMEM((2, 8, 2 * NG * EDGE), F32),
            pltpu.VMEM((2, NG * EDGE, HD), F32),
            dma((3, HEADS)), dma((3, HEADS)), dma((3, HEADS)), dma((3, HEADS)), dma((2, HEADS)), dma((2, HEADS)),
            dma((HEADS,)), dma((HEADS,)), dma((HEADS,)), dma((HEADS,)),
        ],
        compiler_params=pltpu.CompilerParams(collective_id=0, has_side_effects=True, vmem_limit_bytes=56 * 2**20),
    )(edge_cols, query[0], key[0], value[0])
    return out[None]


def solution(mesh):
    spec = P("cam", "seq", None, None)
    return jax.shard_map(local, mesh=mesh, in_specs=(spec, spec, spec, P()), out_specs=spec, check_vma=False)
```

time: 446 us -> 228 us (0.51)
  Pallas kernels: 0 us -> 225 us
  waiting for transfers between devices: 205 us -> 0 us
  blocking collectives: 85.2 us -> 0 us
  local copies, waits for them, and re-layouts: 71.6 us -> 2.39 us
  starting transfers between devices: 48.8 us -> 0 us
  matrix products: 15.8 us -> 0 us
  other arithmetic: 14.3 us -> 0 us
    pallas_call x0 -> x1, Pallas kernels: none -> 225 us  [local(): pl.pallas_call(kernel, out_shape=jax.ShapeDtypeStruct(query.shape[1:], qu...]
    all_to_all x3 -> x0, waiting for transfers between devices: 205 us -> none  [the longest x1 74.6 us: local(): lax.all_to_all(flatten(query), 'seq', split_axis=1, concat_axis=0, tiled=...]
    all_to_all x1 -> x0, blocking collectives: 85.2 us -> none  [local(): lax.all_to_all(outgoing, 'seq', split_axis=0, concat_axis=1, tiled=True)]
    all_to_all x3 -> x0, starting transfers between devices: 34.6 us -> none  [the longest x1 19.6 us: local(): lax.all_to_all(flatten(query), 'seq', split_axis=1, concat_axis=0, tiled=...]
    another operation x9 -> x0, local copies, waits for them, and re-layouts: 19.4 us -> none
    dot_general x6 -> x0, matrix products: 15.8 us -> none  [the longest x3 10.2 us: attend(): jnp.einsum('fhqk,fkhd->fqhd', weights, v_four, preferred_element_type=jnp...]
    ppermute x4 -> x0, starting transfers between devices: 14.2 us -> none  [shifted(): return lax.ppermute(value, axis, pairs)]
    concatenate x12 -> x0, local copies, waits for them, and re-layouts: 12.7 us -> none  [the longest x3 3.4 us: local(): jnp.concatenate([prior_vr, left_cols(v_here)], axis=1)]
  transfers between devices with their start and end apart: 7 -> 0, of which waited for: 3 -> 0; matrix products, arithmetic and copies ran while one was open for 13% -> 0% of each run, Pallas kernels for 0% -> 0%
where the time goes in v1:
time: 228 us
  Pallas kernels  225 us (99%)
  local copies, waits for them, and re-layouts  2.39 us (1%)
    pallas_call x1, Pallas kernels, local(): pl.pallas_call(kernel, out_shape=jax.ShapeDtypeStruct(query.shape[1:], qu...  225 us

profile of v1, /device:TPU:1, one launch (start us, length us, event | category | flops | bytes accessed | tf_op | source)
XLA Modules:
  0.0 227.5 jit_solution(6577286297173470405)
XLA Ops:
  0.0 225.1 %shard_map.46 = bf16[6,64,1536]{2,1,0:T(8,128)(2,1)} custom-call(s32[8]{0:T(128)} %edge_ref.1, bf16[6,64,1536]{2,1,0:T(8,128)(2,1)} %bitcast.5, bf16[6,64,1536]{2,1,0:T(8,128)(2,1)} %bitcast.6, bf16[6,64,1536]{2,1,0:T(8,128)(2,1)} %bitcast.7), custom_call_target="tpu_custom_call" | custom-call | tf_op jit(solution)/shard_map/pallas_call | solution.py:331
  225.1 2.4 %copy.6 = bf16[1,6,64,1536]{3,2,1,0:T(8,128)(2,1)} copy(bf16[1,6,64,1536]{3,2,1,0:T(8,128)(2,1)} %bitcast.4) | data formatting | bytes 2359296

commit v2 on v1

v2 whole, which is shorter than its diff:
```python
import jax
import jax.numpy as jnp
from jax import lax
from jax.experimental import pallas as pl
from jax.experimental.pallas import tpu as pltpu
from jax.sharding import PartitionSpec as P

MESH = pl.DeviceIdType.MESH
HD = 128
COLS = 32
MAX_COLS = 14
BF = jnp.bfloat16
F32 = jnp.float32
NZ = 16
NG = 4
BLK = 6
FR = 16
HEADS = 3
FG = 4
PER = 4
POS = NZ * BLK
EDGE = 48
MID = 16
ROWS_G = 2 * EDGE + MID
ROOMS = (EDGE, EDGE, MID)
SETS = ((0, 2), (2, 1))
AHEAD = 2
SCALE = HD**-0.5 * 1.4426950408889634


def tables():
    slots, cols, counts = [], [], []
    for g in range(NG):
        left, right, mid = [], [], []
        for b in range(PER):
            for i in range(BLK):
                col = (PER * BLK * b + BLK * g + i) % COLS
                entry = (BLK * b + i, col)
                (left if col < MAX_COLS else right if col >= COLS - MAX_COLS else mid).append(entry)
        groups = [left, right, mid]
        counts.append([len(x) for x in groups])
        row_s, row_c = [], []
        for x, room in zip(groups, [room // 4 for room in ROOMS]):
            for k in range(room):
                row_s.append(x[k][0] if k < len(x) else x[0][0])
                row_c.append(x[k][1] if k < len(x) else -1)
        slots.append(row_s)
        cols.append(row_c)
    return slots, cols, counts


SLOTS, COLUMNS, COUNTS = tables()
KINDS = len(SLOTS[0])


def by_g(g, values):
    if len(set(values)) == 1:
        return values[0]
    out = jnp.int32(values[-1])
    for n in range(len(values) - 2, -1, -1):
        out = jnp.where(g == n, jnp.int32(values[n]), out)
    return out


def dot(a, b, dims):
    return lax.dot_general(a, b, (dims, ((), ())), preferred_element_type=F32)


def kernel(
    edge_ref, q_ref, k_ref, v_ref, out_ref,
    rxz_a, st2_a, rx2_a, edges_a, ost_a, rxo_a, otx_a,
    rxz_b, st2_b, rx2_b, edges_b, ost_b, rxo_b, otx_b,
    perm, bias, qvalid,
    z_send, z_recv, g_send, g_recv, e_send, e_recv, og_send, og_recv, oz_send, oz_recv,
):
    cam = lax.axis_index("cam")
    seq = lax.axis_index("seq")
    cams = lax.axis_size("cam")
    z = seq // NG
    g = seq % NG
    prior = lax.rem(cam + cams - 1, cams)
    after = lax.rem(cam + 1, cams)
    hg, fg = z // 4, z % 4
    args = (k_ref, v_ref, q_ref)
    rxz, st2, rx2, edges = (rxz_a, rxz_b), (st2_a, st2_b), (rx2_a, rx2_b), (edges_a, edges_b)
    ost, rxo, otx = (ost_a, ost_b), (rxo_a, rxo_b), (otx_a, otx_b)

    def ring(d):
        return lax.rem(z + d, NZ)

    bar = pltpu.get_barrier_semaphore()

    def greet(dev):
        pl.semaphore_signal(bar, inc=1, device_id=dev, device_id_type=MESH)

    @pl.loop(1, NZ)
    def _(d):
        greet((cam, ring(d) * NG + g))

    for d in range(1, NG):
        greet((cam, z * NG + lax.rem(g + d, NG)))
    for d in range(NG):
        greet((prior, z * NG + d))
        greet((after, z * NG + d))
    pl.semaphore_wait(bar, NZ - 1 + NG - 1 + 2 * NG)

    def lanes_of(zt, s):
        first, count = SETS[s]
        return pl.ds(pl.multiple_of(((zt // 4) * HEADS + first) * HD, HD), count * HD)

    def frames_of(zt):
        return pl.ds(pl.multiple_of((zt % 4) * FR, FR), FR)

    def to_ring(go):
        @pl.loop(1, NZ // 2)
        def _(d):
            go(ring(d))
            go(ring(NZ - d))

        go(ring(NZ // 2))

    def z_issue(chunk):
        s, t = chunk
        dst = rxz[s].at[t, pl.ds(z * BLK, BLK)]

        def src(zt):
            return args[t].at[:, frames_of(zt), lanes_of(zt, s)]

        def go(zt):
            pltpu.make_async_remote_copy(
                src(zt), dst, z_send.at[s, t], z_recv.at[s, t], device_id=(cam, zt * NG + g), device_id_type=MESH
            ).start()

        to_ring(go)
        pltpu.make_async_copy(src(z), dst, z_recv.at[s, t]).start()

    def wait_bytes(ref, sem):
        pltpu.make_async_copy(ref, ref, sem).wait()

    chunks = [(s, t) for s in range(len(SETS)) for t in range(3)]
    for chunk in chunks[:AHEAD]:
        z_issue(chunk)

    r = lax.broadcasted_iota(jnp.int32, (256, 256), 0)
    c = lax.broadcasted_iota(jnp.int32, (256, 256), 1)
    perm[...] = jnp.where(c == (r % 16) * 16 + r // 16, 1.0, 0.0).astype(BF)

    def column_of(idx, kind):
        room = ROOMS[kind]
        dev, k = idx // room, (idx % room) // 4
        col = jnp.full(idx.shape, -1, jnp.int32)
        for n in range(NG):
            for kk in range(COUNTS[n][kind]):
                here = jnp.logical_and(dev == n, k == kk)
                col = jnp.where(here, COLUMNS[n][sum(ROOMS[:kind]) // 4 + kk], col)
        return col

    w_right = edge_ref[cam]
    w_left = edge_ref[prior]

    def on_left(col, w):
        return jnp.logical_and(col >= 0, col < w)

    def on_right(col, w):
        return col >= COLS - w

    lane = lax.broadcasted_iota(jnp.int32, (8, NG * EDGE), 1)
    col_l, col_r = column_of(lane, 0), column_of(lane, 1)
    col_m = column_of(lax.broadcasted_iota(jnp.int32, (8, NG * MID), 1), 2)

    def as_bias(*ok):
        return jnp.concatenate([jnp.where(x, 0.0, -1e30).astype(F32) for x in ok], axis=1)

    bias[0] = as_bias(col_l >= 0, col_r >= 0, col_m >= 0)
    bias[1, :, : 2 * NG * EDGE] = as_bias(on_right(col_r, w_left), on_left(col_l, w_left))
    bias[2, :, : 2 * NG * EDGE] = as_bias(on_right(col_r, w_right), on_left(col_l, w_right))
    row = lax.broadcasted_iota(jnp.int32, (NG * EDGE, HD), 0)
    qvalid[0] = jnp.where(on_left(column_of(row, 0), w_left), 1.0, 0.0).astype(F32)
    qvalid[1] = jnp.where(on_right(column_of(row, 1), w_right), 1.0, 0.0).astype(F32)

    slot = [by_g(g, [SLOTS[n][k] for n in range(NG)]) for k in range(KINDS)]
    kinds = [(kind, k) for kind in range(3) for k in range(ROOMS[kind] // 4)]
    real = [by_g(g, [1 if k < COUNTS[n][kind] else 0 for n in range(NG)]) for kind, k in kinds]

    def place(k, a):
        if isinstance(real[k], int):
            return PER * BLK * a + slot[k]
        return jnp.where(real[k] == 1, PER * BLK * a + slot[k], POS)

    def to_frames(s, t):
        for j in range(KINDS // 4):
            x = jnp.concatenate(
                [rxz[s][t, PER * BLK * a + slot[k]] for k in range(4 * j, 4 * j + 4) for a in range(4)], axis=0
            )
            y = dot(perm[...], x, ((1,), (0,))).astype(BF)
            st2[s][t, :, 16 * j : 16 * j + 16, :] = y.reshape(FR, 16, x.shape[1])

    def to_tiles(s):
        for j in range(KINDS // 4):
            x = rxo[s][:, 16 * j : 16 * j + 16, :]
            x = x.reshape(256, x.shape[2])
            y = dot(perm[...], x, ((1,), (0,))).astype(BF).reshape(16, FR, x.shape[1])
            for n in range(16):
                otx[s][place(4 * j + n // 4, n % 4)] = y[n]

    def g_issue(s, t):
        for d in (2, 1, 3):
            gt = lax.rem(g + d, NG)
            pltpu.make_async_remote_copy(
                st2[s].at[t, pl.ds(gt * FG, FG)], rx2[s].at[t, g], g_send.at[s, t], g_recv.at[s, t],
                device_id=(cam, z * NG + gt), device_id_type=MESH,
            ).start()
        pltpu.make_async_copy(st2[s].at[t, pl.ds(g * FG, FG)], rx2[s].at[t, g], g_recv.at[s, t]).start()
        if t < 2:
            for d in range(NG):
                gt = lax.rem(g + d, NG)
                for side, who, base in ((0, after, EDGE), (1, prior, 0)):
                    pltpu.make_async_remote_copy(
                        st2[s].at[t, pl.ds(gt * FG, FG), pl.ds(base, EDGE)], edges[s].at[t, side, g],
                        e_send.at[s, t], e_recv.at[s, t],
                        device_id=(who, z * NG + gt), device_id_type=MESH,
                    ).start()

    def arrive(n):
        s, t = chunks[n]
        wait_bytes(rxz[s].at[t], z_recv.at[s, t])
        if n + AHEAD < len(chunks):
            z_issue(chunks[n + AHEAD])
        to_frames(s, t)
        g_issue(s, t)

    def weigh(q, k, v, extra):
        x = dot(q, k, ((1,), (1,))) * SCALE + extra
        p = jnp.exp2(x - jnp.max(x, axis=-1, keepdims=True))
        w = (p * (1.0 / jnp.sum(p, axis=-1, keepdims=True))).astype(BF)
        return dot(w, v, ((1,), (0,)))

    def attend(s):
        for t in range(3):
            wait_bytes(rx2[s].at[t], g_recv.at[s, t])
        for t in range(2):
            wait_bytes(edges[s].at[t], e_recv.at[s, t])
        count = SETS[s][1]

        @pl.loop(0, FG * count)
        def _(n):
            f, h = n // count, n % count
            lanes = pl.ds(pl.multiple_of(h * HD, HD), HD)

            def gather(t):
                parts, lo = [], 0
                for room in ROOMS:
                    parts.append([rx2[s][t, gs, f, lo : lo + room, lanes] for gs in range(NG)])
                    lo += room
                return [jnp.concatenate(x, axis=0) for x in parts]

            def edge(t, side):
                return jnp.concatenate([edges[s][t, side, gs, f, :, lanes] for gs in range(NG)], axis=0)

            (kl, kr, km), (vl, vr, vm), (ql, qr, qm) = gather(0), gather(1), gather(2)
            k_all, v_all = jnp.concatenate([kl, kr, km], axis=0), jnp.concatenate([vl, vr, vm], axis=0)
            k_left, v_left = jnp.concatenate([edge(0, 0), kl], axis=0), jnp.concatenate([edge(1, 0), vl], axis=0)
            k_right, v_right = jnp.concatenate([kr, edge(0, 1)], axis=0), jnp.concatenate([vr, edge(1, 1)], axis=0)
            here, joint_l, joint_r = bias[0, 0:1], bias[1, 0:1, : 2 * NG * EDGE], bias[2, 0:1, : 2 * NG * EDGE]
            o_l = weigh(ql, k_all, v_all, here) + weigh(ql, k_left, v_left, joint_l) * qvalid[0]
            o_r = weigh(qr, k_all, v_all, here) + weigh(qr, k_right, v_right, joint_r) * qvalid[1]
            o_m = weigh(qm, k_all, v_all, here)
            o_l, o_r, o_m = o_l.astype(BF), o_r.astype(BF), o_m.astype(BF)
            for gs in range(NG):
                ost[s][gs, f, 0:EDGE, lanes] = o_l[gs * EDGE : (gs + 1) * EDGE]
                ost[s][gs, f, EDGE : 2 * EDGE, lanes] = o_r[gs * EDGE : (gs + 1) * EDGE]
                ost[s][gs, f, 2 * EDGE :, lanes] = o_m[gs * MID : (gs + 1) * MID]
            for d in (2, 1, 3):
                gt = lax.rem(g + d, NG)
                pltpu.make_async_remote_copy(
                    ost[s].at[gt, f, :, lanes], rxo[s].at[g * FG + f, :, lanes], og_send.at[s], og_recv.at[s],
                    device_id=(cam, z * NG + gt), device_id_type=MESH,
                ).start()
            pltpu.make_async_copy(
                ost[s].at[g, f, :, lanes], rxo[s].at[g * FG + f, :, lanes], og_recv.at[s]
            ).start()

    def give_back(s):
        wait_bytes(rxo[s], og_recv.at[s])
        to_tiles(s)
        dst = out_ref.at[:, frames_of(z), lanes_of(z, s)]

        def go(zt):
            pltpu.make_async_remote_copy(
                otx[s].at[pl.ds(zt * BLK, BLK)], dst, oz_send.at[s], oz_recv.at[s],
                device_id=(cam, zt * NG + g), device_id_type=MESH,
            ).start()

        to_ring(go)
        pltpu.make_async_copy(otx[s].at[pl.ds(z * BLK, BLK)], dst, oz_recv.at[s]).start()

    arrive(0)
    arrive(1)
    arrive(2)
    arrive(3)
    attend(0)
    arrive(4)
    give_back(0)
    arrive(5)
    attend(1)
    give_back(1)

    for s in range(len(SETS)):
        for t in range(3):
            wait_bytes(rxz[s].at[t, pl.ds(0, (NZ - 1) * BLK)], z_send.at[s, t])
            wait_bytes(rx2[s].at[t, pl.ds(0, NG - 1)], g_send.at[s, t])
        for t in range(2):
            wait_bytes(edges[s].at[t], e_send.at[s, t])
        wait_bytes(ost[s].at[pl.ds(0, NG - 1)], og_send.at[s])
        wait_bytes(rxz[s].at[0, pl.ds(0, (NZ - 1) * BLK)], oz_send.at[s])
        wait_bytes(rxz[s].at[0], oz_recv.at[s])


def local(query, key, value, edge_cols):
    sems = [(2, 3)] * 4 + [(2, 2)] * 2 + [(2,)] * 4
    buffers = []
    for _, count in SETS:
        wide = count * HD
        for shape in (
            (3, POS, FR), (3, FR, ROWS_G), (3, NG, FG, ROWS_G), (2, 2, NG, FG, EDGE), (NG, FG, ROWS_G), (FR, ROWS_G), (POS + 1, FR)
        ):
            buffers.append(pltpu.VMEM(shape + (wide,), BF))
    out = pl.pallas_call(
        kernel,
        out_shape=jax.ShapeDtypeStruct(query.shape[1:], query.dtype),
        in_specs=[pl.BlockSpec(memory_space=pltpu.SMEM)] + [pl.BlockSpec(memory_space=pl.ANY)] * 3,
        out_specs=pl.BlockSpec(memory_space=pl.ANY),
        scratch_shapes=buffers
        + [pltpu.VMEM((256, 256), BF), pltpu.VMEM((3, 8, NG * ROWS_G), F32), pltpu.VMEM((2, NG * EDGE, HD), F32)]
        + [pltpu.SemaphoreType.DMA(shape) for shape in sems],
        compiler_params=pltpu.CompilerParams(collective_id=0, has_side_effects=True, vmem_limit_bytes=52 * 2**20),
    )(edge_cols, query[0], key[0], value[0])
    return out[None]


def solution(mesh):
    spec = P("cam", "seq", None, None)
    return jax.shard_map(local, mesh=mesh, in_specs=(spec, spec, spec, P()), out_specs=spec, check_vma=False)
```

time: 228 us -> 226 us (level)
  no operation moved by 1% of the time
where the time goes in v2:
time: 226 us
  Pallas kernels  224 us (99%)
    pallas_call x1, Pallas kernels, local(): pl.pallas_call(kernel, out_shape=jax.ShapeDtypeStruct(query.shape[1:], qu...  224 us

profile of v2, /device:TPU:1, one launch (start us, length us, event | category | flops | bytes accessed | tf_op | source)
XLA Modules:
  0.0 225.8 jit_solution(9604942758918116775)
XLA Ops:
  0.0 0.0 copy-start
  0.0 0.7 copy-done
  0.7 224.1 %shard_map.46 = bf16[6,64,1536]{2,1,0:T(8,128)(2,1)S(1)} custom-call(s32[8]{0:T(128)S(1)} %copy-done, bf16[6,64,1536]{2,1,0:T(8,128)(2,1)} %bitcast.5, bf16[6,64,1536]{2,1,0:T(8,128)(2,1)} %bitcast.6, bf16[6,64,1536]{2,1,0:T(8,128)(2,1)} %bitcast.7), custom_call_target="tpu_custom_call" | custom-call | tf_op jit(solution)/shard_map/pallas_call | solution.py:328
  224.7 1.0 copy.6
Async XLA Ops:
  0.0 0.7 copy-start

commit v3 on v2

--- a/solution.py
+++ b/solution.py
@@ -25,6 +25,7 @@
 ROOMS = (EDGE, EDGE, MID)
 SETS = ((0, 2), (2, 1))
 AHEAD = 2
+FIRST = 4
 SCALE = HD**-0.5 * 1.4426950408889634
 
 
@@ -118,6 +119,19 @@
             go(ring(NZ - d))
 
         go(ring(NZ // 2))
+
+    def back_to_ring(go):
+        def go_if(ok, zt):
+            pl.when(ok)(lambda: go(zt))
+
+        @pl.loop(1, NZ // 2)
+        def _(d):
+            zt = lax.rem(z + d, FIRST)
+            go_if(jnp.logical_and(d <= FIRST, zt != z), zt)
+            go_if(ring(d) >= FIRST, ring(d))
+            go_if(ring(NZ - d) >= FIRST, ring(NZ - d))
+
+        go_if(ring(NZ // 2) >= FIRST, ring(NZ // 2))
 
     def z_issue(chunk):
         s, t = chunk
@@ -291,7 +305,7 @@
                 device_id=(cam, zt * NG + g), device_id_type=MESH,
             ).start()
 
-        to_ring(go)
+        back_to_ring(go)
         pltpu.make_async_copy(otx[s].at[pl.ds(z * BLK, BLK)], dst, oz_recv.at[s]).start()
 
     arrive(0)

time: 226 us -> 221 us (0.978); the launches traced: 226 us -> 217 us
  Pallas kernels: 224 us -> 215 us
    pallas_call x1, Pallas kernels: 224 us -> 215 us  [local(): pl.pallas_call(kernel, out_shape=jax.ShapeDtypeStruct(query.shape[1:], qu...]
where the time goes in v3:
time: 221 us; the launch traced here: 217 us
  Pallas kernels  215 us (97%)
    pallas_call x1, Pallas kernels, local(): pl.pallas_call(kernel, out_shape=jax.ShapeDtypeStruct(query.shape[1:], qu...  215 us

profile of v3, /device:TPU:1, one launch (start us, length us, event | category | flops | bytes accessed | tf_op | source)
XLA Modules:
  0.0 217.0 jit_solution(15879899900674165296)
XLA Ops:
  0.0 0.0 copy-start
  0.0 0.7 copy-done
  0.7 215.3 %shard_map.46 = bf16[6,64,1536]{2,1,0:T(8,128)(2,1)S(1)} custom-call(s32[8]{0:T(128)S(1)} %copy-done, bf16[6,64,1536]{2,1,0:T(8,128)(2,1)} %bitcast.5, bf16[6,64,1536]{2,1,0:T(8,128)(2,1)} %bitcast.6, bf16[6,64,1536]{2,1,0:T(8,128)(2,1)} %bitcast.7), custom_call_target="tpu_custom_call" | custom-call | tf_op jit(solution)/shard_map/pallas_call | solution.py:342
  216.0 1.0 copy.6
Async XLA Ops:
  0.0 0.7 copy-start

commit v4 on v3

--- a/solution.py
+++ b/solution.py
@@ -69,10 +69,10 @@
 
 def kernel(
     edge_ref, q_ref, k_ref, v_ref, out_ref,
-    rxz_a, st2_a, rx2_a, edges_a, ost_a, rxo_a, otx_a,
-    rxz_b, st2_b, rx2_b, edges_b, ost_b, rxo_b, otx_b,
+    tx_a, rkv_a, rq_a, st2_a, rx2_a, edges_a, ost_a, rxo_a, otx_a,
+    tx_b, rkv_b, rq_b, st2_b, rx2_b, edges_b, ost_b, rxo_b, otx_b,
     perm, bias, qvalid,
-    z_send, z_recv, g_send, g_recv, e_send, e_recv, og_send, og_recv, oz_send, oz_recv,
+    stage, z_send, z_recv, g_send, g_recv, e_send, e_recv, og_send, og_recv, oz_send, oz_recv,
 ):
     cam = lax.axis_index("cam")
     seq = lax.axis_index("seq")
@@ -83,11 +83,23 @@
     after = lax.rem(cam + 1, cams)
     hg, fg = z // 4, z % 4
     args = (k_ref, v_ref, q_ref)
-    rxz, st2, rx2, edges = (rxz_a, rxz_b), (st2_a, st2_b), (rx2_a, rx2_b), (edges_a, edges_b)
+    tx, rxz = (tx_a, tx_b), ((rkv_a, rq_a), (rkv_b, rq_b))
+    st2, rx2, edges = (st2_a, st2_b), (rx2_a, rx2_b), (edges_a, edges_b)
     ost, rxo, otx = (ost_a, ost_b), (rxo_a, rxo_b), (otx_a, otx_b)
 
     def ring(d):
         return lax.rem(z + d, NZ)
+
+    def lanes_at(hgt, s):
+        first, count = SETS[s]
+        return pl.ds(pl.multiple_of((hgt * HEADS + first) * HD, HD), count * HD)
+
+    def gather_kv(s):
+        for n in range(NZ // 4):
+            for t in range(2):
+                pltpu.make_async_copy(args[t].at[:, :, lanes_at(n, s)], tx[s].at[n, t], stage.at[s]).start()
+
+    gather_kv(0)
 
     bar = pltpu.get_barrier_semaphore()
 
@@ -106,8 +118,7 @@
     pl.semaphore_wait(bar, NZ - 1 + NG - 1 + 2 * NG)
 
     def lanes_of(zt, s):
-        first, count = SETS[s]
-        return pl.ds(pl.multiple_of(((zt // 4) * HEADS + first) * HD, HD), count * HD)
+        return lanes_at(zt // 4, s)
 
     def frames_of(zt):
         return pl.ds(pl.multiple_of((zt % 4) * FR, FR), FR)
@@ -126,34 +137,40 @@
 
         @pl.loop(1, NZ // 2)
         def _(d):
-            zt = lax.rem(z + d, FIRST)
+            zt = lax.rem(d - 1 + (g % 2) * (z + 1), FIRST)
             go_if(jnp.logical_and(d <= FIRST, zt != z), zt)
             go_if(ring(d) >= FIRST, ring(d))
             go_if(ring(NZ - d) >= FIRST, ring(NZ - d))
 
         go_if(ring(NZ // 2) >= FIRST, ring(NZ // 2))
 
+    def wait_bytes(ref, sem):
+        pltpu.make_async_copy(ref, ref, sem).wait()
+
     def z_issue(chunk):
-        s, t = chunk
-        dst = rxz[s].at[t, pl.ds(z * BLK, BLK)]
+        s, part = chunk
+        dst = rxz[s][part].at[z]
+        if part == 0:
+            wait_bytes(tx[s], stage.at[s])
 
         def src(zt):
-            return args[t].at[:, frames_of(zt), lanes_of(zt, s)]
+            if part == 0:
+                return tx[s].at[zt // 4, :, :, frames_of(zt)]
+            return q_ref.at[:, frames_of(zt), lanes_of(zt, s)]
 
         def go(zt):
             pltpu.make_async_remote_copy(
-                src(zt), dst, z_send.at[s, t], z_recv.at[s, t], device_id=(cam, zt * NG + g), device_id_type=MESH
+                src(zt), dst, z_send.at[s, part], z_recv.at[s, part],
+                device_id=(cam, zt * NG + g), device_id_type=MESH,
             ).start()
 
         to_ring(go)
-        pltpu.make_async_copy(src(z), dst, z_recv.at[s, t]).start()
-
-    def wait_bytes(ref, sem):
-        pltpu.make_async_copy(ref, ref, sem).wait()
-
-    chunks = [(s, t) for s in range(len(SETS)) for t in range(3)]
+        pltpu.make_async_copy(src(z), dst, z_recv.at[s, part]).start()
+
+    chunks = [(s, part) for s in range(len(SETS)) for part in range(2)]
     for chunk in chunks[:AHEAD]:
         z_issue(chunk)
+    gather_kv(1)
 
     r = lax.broadcasted_iota(jnp.int32, (256, 256), 0)
     c = lax.broadcasted_iota(jnp.int32, (256, 256), 1)
@@ -193,6 +210,8 @@
     qvalid[1] = jnp.where(on_right(column_of(row, 1), w_right), 1.0, 0.0).astype(F32)
 
     slot = [by_g(g, [SLOTS[n][k] for n in range(NG)]) for k in range(KINDS)]
+    slot_z = [by_g(g, [SLOTS[n][k] // BLK for n in range(NG)]) for k in range(KINDS)]
+    slot_i = [by_g(g, [SLOTS[n][k] % BLK for n in range(NG)]) for k in range(KINDS)]
     kinds = [(kind, k) for kind in range(3) for k in range(ROOMS[kind] // 4)]
     real = [by_g(g, [1 if k < COUNTS[n][kind] else 0 for n in range(NG)]) for kind, k in kinds]
 
@@ -203,9 +222,12 @@
 
     def to_frames(s, t):
         for j in range(KINDS // 4):
-            x = jnp.concatenate(
-                [rxz[s][t, PER * BLK * a + slot[k]] for k in range(4 * j, 4 * j + 4) for a in range(4)], axis=0
-            )
+            tiles = []
+            for k in range(4 * j, 4 * j + 4):
+                for a in range(4):
+                    where = (PER * a + slot_z[k], slot_i[k])
+                    tiles.append(rxz[s][1][where] if t == 2 else rxz[s][0][where[0], t, where[1]])
+            x = jnp.concatenate(tiles, axis=0)
             y = dot(perm[...], x, ((1,), (0,))).astype(BF)
             st2[s][t, :, 16 * j : 16 * j + 16, :] = y.reshape(FR, 16, x.shape[1])
 
@@ -236,12 +258,13 @@
                     ).start()
 
     def arrive(n):
-        s, t = chunks[n]
-        wait_bytes(rxz[s].at[t], z_recv.at[s, t])
+        s, part = chunks[n]
+        wait_bytes(rxz[s][part], z_recv.at[s, part])
         if n + AHEAD < len(chunks):
             z_issue(chunks[n + AHEAD])
-        to_frames(s, t)
-        g_issue(s, t)
+        for t in ((0, 1), (2,))[part]:
+            to_frames(s, t)
+            g_issue(s, t)
 
     def weigh(q, k, v, extra):
         x = dot(q, k, ((1,), (1,))) * SCALE + extra
@@ -310,33 +333,32 @@
 
     arrive(0)
     arrive(1)
+    attend(0)
     arrive(2)
+    give_back(0)
     arrive(3)
-    attend(0)
-    arrive(4)
-    give_back(0)
-    arrive(5)
     attend(1)
     give_back(1)
 
     for s in range(len(SETS)):
         for t in range(3):
-            wait_bytes(rxz[s].at[t, pl.ds(0, (NZ - 1) * BLK)], z_send.at[s, t])
             wait_bytes(rx2[s].at[t, pl.ds(0, NG - 1)], g_send.at[s, t])
         for t in range(2):
             wait_bytes(edges[s].at[t], e_send.at[s, t])
         wait_bytes(ost[s].at[pl.ds(0, NG - 1)], og_send.at[s])
-        wait_bytes(rxz[s].at[0, pl.ds(0, (NZ - 1) * BLK)], oz_send.at[s])
-        wait_bytes(rxz[s].at[0], oz_recv.at[s])
+        for part in range(2):
+            wait_bytes(rxz[s][part].at[pl.ds(0, NZ - 1)], z_send.at[s, part])
+        wait_bytes(rxz[s][1].at[pl.ds(0, NZ - 1)], oz_send.at[s])
+        wait_bytes(rxz[s][1], oz_recv.at[s])
 
 
 def local(query, key, value, edge_cols):
-    sems = [(2, 3)] * 4 + [(2, 2)] * 2 + [(2,)] * 4
+    sems = [(2,)] + [(2, 2)] * 2 + [(2, 3)] * 2 + [(2, 2)] * 2 + [(2,)] * 4
     buffers = []
     for _, count in SETS:
         wide = count * HD
         for shape in (
-            (3, POS, FR), (3, FR, ROWS_G), (3, NG, FG, ROWS_G), (2, 2, NG, FG, EDGE), (NG, FG, ROWS_G), (FR, ROWS_G), (POS + 1, FR)
+            (NZ // 4, 2, BLK, query.shape[2]), (NZ, 2, BLK, FR), (NZ, BLK, FR), (3, FR, ROWS_G), (3, NG, FG, ROWS_G), (2, 2, NG, FG, EDGE), (NG, FG, ROWS_G), (FR, ROWS_G), (POS + 1, FR)
         ):
             buffers.append(pltpu.VMEM(shape + (wide,), BF))
     out = pl.pallas_call(

time: 221 us -> 220 us (level)
  no operation moved by 1% of the time
where the time goes in v4:
time: 220 us; the launch traced here: 217 us
  Pallas kernels  215 us (98%)
    pallas_call x1, Pallas kernels, local(): pl.pallas_call(kernel, out_shape=jax.ShapeDtypeStruct(query.shape[1:], qu...  215 us

profile of v4, /device:TPU:1, one launch (start us, length us, event | category | flops | bytes accessed | tf_op | source)
XLA Modules:
  0.0 217.1 jit_solution(14024232313601479397)
XLA Ops:
  0.0 0.0 copy-start
  0.0 0.7 copy-done
  0.7 215.5 %shard_map.46 = bf16[6,64,1536]{2,1,0:T(8,128)(2,1)S(1)} custom-call(s32[8]{0:T(128)S(1)} %copy-done, bf16[6,64,1536]{2,1,0:T(8,128)(2,1)} %bitcast.5, bf16[6,64,1536]{2,1,0:T(8,128)(2,1)} %bitcast.6, bf16[6,64,1536]{2,1,0:T(8,128)(2,1)} %bitcast.7), custom_call_target="tpu_custom_call" | custom-call | tf_op jit(solution)/shard_map/pallas_call | solution.py:364
  216.1 1.0 copy.6
Async XLA Ops:
  0.0 0.7 copy-start

commit v5 on v4

--- a/solution.py
+++ b/solution.py
@@ -99,8 +99,6 @@
             for t in range(2):
                 pltpu.make_async_copy(args[t].at[:, :, lanes_at(n, s)], tx[s].at[n, t], stage.at[s]).start()
 
-    gather_kv(0)
-
     bar = pltpu.get_barrier_semaphore()
 
     def greet(dev):
@@ -115,6 +113,7 @@
     for d in range(NG):
         greet((prior, z * NG + d))
         greet((after, z * NG + d))
+    gather_kv(0)
     pl.semaphore_wait(bar, NZ - 1 + NG - 1 + 2 * NG)
 
     def lanes_of(zt, s):

time: 220 us -> 220 us (level)
  no operation moved by 1% of the time
where the time goes in v5:
time: 220 us; the launch traced here: 217 us
  Pallas kernels  215 us (98%)
    pallas_call x1, Pallas kernels, local(): pl.pallas_call(kernel, out_shape=jax.ShapeDtypeStruct(query.shape[1:], qu...  215 us

profile of v5, /device:TPU:1, one launch (start us, length us, event | category | flops | bytes accessed | tf_op | source)
XLA Modules:
  0.0 217.1 jit_solution(13983043580159965106)
XLA Ops:
  0.0 0.0 copy-start
  0.0 0.7 copy-done
  0.7 215.5 %shard_map.46 = bf16[6,64,1536]{2,1,0:T(8,128)(2,1)S(1)} custom-call(s32[8]{0:T(128)S(1)} %copy-done, bf16[6,64,1536]{2,1,0:T(8,128)(2,1)} %bitcast.5, bf16[6,64,1536]{2,1,0:T(8,128)(2,1)} %bitcast.6, bf16[6,64,1536]{2,1,0:T(8,128)(2,1)} %bitcast.7), custom_call_target="tpu_custom_call" | custom-call | tf_op jit(solution)/shard_map/pallas_call | solution.py:363
  216.1 1.0 copy.6
Async XLA Ops:
  0.0 0.7 copy-start
